TPU v7x, 256 devices: a whole 4x4x8 slice. The times are simulated.
256 devices in a mesh: section: 2 (over y_hi), row: 16 (over z, y_lo), col: 8 (over x, core).
Axes of the slice: x: 4, y: 4 (y_hi: 2, y_lo: 2; y = y_hi * 2 + y_lo), z: 8, core: 2. Of those that a mesh axis runs over, the one named last changes fastest.
Arguments:
- handed: bfloat16 [2, 768, 768, 128], P('section', ('row', 'col')), may hold values from -6 to 6
- residue_mask: int32 [2, 768], P('section'), may hold values 0 or 1
- input_weights: bfloat16 [2, 128, 640], P('section'), may hold values from -0.5 to 0.5
- input_gain: float32 [2, 128], P('section'), may hold values from 0.1 to 1.9
- product_gain: float32 [2, 128], P('section'), may hold values from 0.1 to 1.9
- output_weights: bfloat16 [2, 128, 128], P('section'), may hold values from -0.5 to 0.5
Outputs:
- updated: bfloat16 [2, 768, 768, 128], P('section', 'row', 'col')
All inputs are finite; a program needn't handle non-finite values. No bound on the sum of `residue_mask` on one device may be relied on, other than what follows from the above.
Results may differ from a plain program's by a relative error of at most 0.0052.
Values may be sent and summed in bfloat16 or wider, within the bound.
A program may use at most 64 MiB of HBM per device.

v0:
```python
import jax
import jax.numpy as jnp
from jax import lax
from jax.sharding import PartitionSpec as P

EPS = 1e-05


def from_behind(shard, axis, by):
    size = lax.axis_size(axis)
    return lax.ppermute(shard, axis, [(i, (i + by) % size) for i in range(size)])


def norm_rows(values, gain):
    center = jnp.mean(values, axis=-1, keepdims=True)
    deviate = values - center
    spread = jnp.mean(deviate * deviate, axis=-1, keepdims=True)
    return deviate * lax.rsqrt(spread + EPS) * gain


def factors(normed, ab_columns, pair_mask, hidden):
    projected = lax.dot_general(
        ab_columns, normed, (((0,), (1,)), ((), ())), preferred_element_type=jnp.float32
    )
    projected = projected.reshape((4, hidden) + pair_mask.shape)
    left_factor = jax.nn.sigmoid(projected[0]) * projected[1] * pair_mask
    right_factor = jax.nn.sigmoid(projected[2]) * projected[3] * pair_mask
    return jnp.stack([left_factor, right_factor]).astype(jnp.bfloat16)


def channel_products(owned):
    return jnp.einsum(
        "hik,hjk->hij", owned[0], owned[1], preferred_element_type=jnp.float32
    ).astype(jnp.bfloat16)


def local(handed, residue_mask, input_weights, input_gain, product_gain, output_weights):
    arrived, present = from_behind((handed, residue_mask.astype(jnp.bfloat16)), "section", 1)
    arrived = arrived[0]
    present = present[0].astype(jnp.float32)
    weights = input_weights[0]
    last_weights = output_weights[0]
    first_gain = input_gain[0]
    second_gain = product_gain[0]
    hidden = last_weights.shape[0]
    channels = arrived.shape[2]
    ab_columns = weights[:, : 4 * hidden]
    gate_columns = weights[:, 4 * hidden :]
    blocked = lax.all_to_all(arrived, "col", split_axis=1, concat_axis=0, tiled=True)
    row_count = blocked.shape[0]
    col_count = blocked.shape[1]
    row_offset = lax.axis_index("row") * row_count
    col_offset = lax.axis_index("col") * col_count
    block_norm = (
        norm_rows(blocked.astype(jnp.float32), first_gain)
        .astype(jnp.bfloat16)
        .reshape(-1, channels)
    )
    gating = jnp.dot(block_norm, gate_columns, preferred_element_type=jnp.float32)
    row_flags = lax.dynamic_slice_in_dim(present, row_offset, row_count, 0)
    col_flags = lax.dynamic_slice_in_dim(present, col_offset, col_count, 0)
    pair_mask = row_flags[:, None] * col_flags[None, :]
    stacked = factors(block_norm, ab_columns, pair_mask, hidden)
    owned = lax.all_to_all(
        lax.all_to_all(stacked, "row", split_axis=1, concat_axis=2, tiled=True),
        "col",
        split_axis=1,
        concat_axis=3,
        tiled=True,
    )
    products_grid = lax.all_to_all(
        lax.all_to_all(channel_products(owned), "col", split_axis=2, concat_axis=0, tiled=True),
        "row",
        split_axis=1,
        concat_axis=0,
        tiled=True,
    )
    widened = products_grid.astype(jnp.float32)
    center = jnp.mean(widened, axis=0, keepdims=True)
    deviate = widened - center
    spread = jnp.mean(deviate * deviate, axis=0, keepdims=True)
    prod_norm = (deviate * lax.rsqrt(spread + EPS) * second_gain[:, None, None]).astype(
        jnp.bfloat16
    )
    prod_norm = prod_norm.reshape(hidden, -1)
    update = lax.dot_general(
        prod_norm, last_weights, (((0,), (0,)), ((), ())), preferred_element_type=jnp.float32
    )
    result = blocked.astype(jnp.float32).reshape(-1, channels) + jax.nn.sigmoid(gating) * update
    return result.astype(jnp.bfloat16).reshape(1, row_count, col_count, channels)


def solution(mesh):
    placed = (
        P("section", ("row", "col"), None, None),
        P("section", None),
        P("section", None, None),
        P("section", None),
        P("section", None),
        P("section", None, None),
    )
    return jax.shard_map(
        local,
        mesh=mesh,
        in_specs=placed,
        out_specs=P("section", "row", "col", None),
        check_vma=False,
    )
```

profile of v0, /device:TPU:1, one launch (start us, length us, event | category | flops | bytes accessed | tf_op | source)
XLA Modules:
  0.0 312.6 jit_solution(4138214229407861593)
XLA Ops:
  0.0 3.7 %collective-permute-start = (bf16[1,6,768,128]{3,2,1,0:T(8,128)(2,1)}, bf16[1,6,768,128]{3,2,1,0:T(8,128)(2,1)S(1)}, u32[]{:S(2)}, u32[]{:S(2)}) collective-permute-start(bf16[1,6,768,128]{3,2,1,0:T(8,128)(2,1)} %param.6), channel_id=1, source_target_pairs={{0,128},{128,0},{1,129},{129,1},{2,130},{130,2},{3,131},{131,3},{4... | collective-permute-start | bytes 3538952 | tf_op jit(solution)/shard_map/ppermute | solution.py:11
  3.7 25.0 %collective-permute-done = bf16[1,6,768,128]{3,2,1,0:T(8,128)(2,1)S(1)} collective-permute-done((bf16[1,6,768,128]{3,2,1,0:T(8,128)(2,1)}, bf16[1,6,768,128]{3,2,1,0:T(8,128)(2,1)S(1)}, u32[]{:S(2)}, u32[]{:S(2)}) %collective-permute-start) | collective-permute-done | bytes 1179680 | tf_op jit(solution)/shard_map/ppermute | solution.py:11
  28.7 2.0 copy.38
  30.7 6.5 %all-to-all-start = ((bf16[6,768,128]{2,0,1:T(8,128)(2,1)}), bf16[6,768,128]{2,0,1:T(8,128)(2,1)S(1)}, u32[]{:S(2)}, u32[]{:S(2)}) async-start(bf16[6,768,128]{2,0,1:T(8,128)(2,1)} %copy.38), calls=%async_computation | async-start | bytes 3145728 | tf_op jit(solution)/shard_map/all_to_all | solution.py:49
  37.2 3.0 collective-permute-start.1
  41.8 16.1 %all-to-all-done = bf16[6,768,128]{2,0,1:T(8,128)(2,1)S(1)} async-done(((bf16[6,768,128]{2,0,1:T(8,128)(2,1)}), bf16[6,768,128]{2,0,1:T(8,128)(2,1)S(1)}, u32[]{:S(2)}, u32[]{:S(2)}) %all-to-all-start) | async-done | bytes 1179680 | tf_op jit(solution)/shard_map/all_to_all | solution.py:49
  59.1 2.3 bitcast_reduce_fusion
  61.5 1.6 fusion.22
  63.2 2.5 fusion.20
  66.8 1.4 convolution_bitcast_fusion
  68.2 3.3 %slice_multiply_fusion.1 = (f32[128,4608]{0,1:T(8,128)}, f32[128,4608]{0,1:T(8,128)}) fusion(f32[512,4608]{0,1:T(8,128)S(1)} %convolution_bitcast_fusion), kind=kLoop, calls=%fused_computation.24 | loop fusion | flops 4718592 | bytes 14155776 | tf_op jit(solution)/shard_map/mul | solution.py:26
  71.5 3.4 %copy.40 = f32[1,128,48,96]{3,2,0,1:T(8,128)} copy(f32[1,128,48,96]{1,3,2,0:T(8,128)} %bitcast.91) | data formatting | bytes 4718592 | tf_op jit(solution)/shard_map/mul | solution.py:26
  75.0 3.5 %copy.41 = f32[1,128,48,96]{3,2,0,1:T(8,128)} copy(f32[1,128,48,96]{1,3,2,0:T(8,128)} %bitcast.90) | data formatting | bytes 4718592 | tf_op jit(solution)/shard_map/mul | solution.py:27
  78.4 3.3 %multiply_convert_fusion.1 = (bf16[1,128,48,96]{3,2,0,1:T(8,128)(2,1)S(1)}, bf16[1,128,48,96]{3,2,0,1:T(8,128)(2,1)S(1)}) fusion(f32[1,128,48,96]{3,2,0,1:T(8,128)} %copy.40, f32[48,96]{1,0:T(8,128)S(1)} %broadcast_multiply_fusion.2, f32[1,128,48,96]{3,2,0,1:T(8,128)} %copy.41), kind=kLoop, calls=%fused_computation.18 | loop fusion | flops 2359296 | bytes 7096320 | tf_op jit(solution)/shard_map/convert.7
  82.4 81.0 %all_to_all.69 = bf16[2,128,48,96]{3,2,0,1:T(8,128)(2,1)S(1)} all-to-all(bf16[2,128,48,96]{3,2,0,1:T(8,128)(2,1)S(1)} %pad_maximum_fusion), channel_id=1, replica_groups=mesh['section'=2,'row'=16,'col'=8] {'row'}, dimensions={1} | all-to-all | bytes 4718592 | tf_op jit(solution)/shard_map/all_to_all | solution.py:65
  163.3 2.5 copy.43
  165.8 4.5 %copy.44 = bf16[2,8,768,96]{2,3,0,1:T(8,128)(2,1)} copy(bf16[2,8,768,96]{3,2,1,0:T(8,128)(2,1)} %bitcast.89) | data formatting | bytes 4718592 | tf_op jit(solution)/shard_map/all_to_all | solution.py:65
  170.3 35.3 %all_to_all.70 = bf16[2,8,768,96]{2,3,0,1:T(8,128)(2,1)S(1)} all-to-all(bf16[2,8,768,96]{2,3,0,1:T(8,128)(2,1)} %copy.44), channel_id=1, replica_groups=mesh['section'=2,'row'=16,'col'=8] {'col'}, dimensions={1} | all-to-all | bytes 4718592 | tf_op jit(solution)/shard_map/all_to_all | solution.py:64
  205.8 2.1 fusion.23
  207.9 6.6 %copy.46 = bf16[1,768,768]{1,0,2:T(2,128)(2,1)} copy(bf16[1,768,768]{2,1,0:T(8,128)(2,1)} %fusion.23) | data formatting | bytes 2359296 | tf_op jit(solution)/shard_map/convert_element_type | solution.py:34
  215.0 9.8 %reduce.8 = bf16[768,768]{1,0:T(8,128)(2,1)} reduce(bf16[768,1,768]{2,1,0:T(2,128)(2,1)} %bitcast.92, bf16[]{:T(256)} %broadcast.154), dimensions={1}, to_apply=%bitcast.78.reduce_sub_computation | reduce | bytes 2359298
  224.8 2.2 reshape.234
  227.0 21.9 %all_to_all.71 = bf16[8,2,36864]{2,1,0:T(2,128)(2,1)} all-to-all(bf16[8,2,36864]{2,1,0:T(2,128)(2,1)} %reshape.234), channel_id=1, replica_groups=mesh['section'=2,'row'=16,'col'=8] {'col'}, dimensions={0} | all-to-all | bytes 2359296 | tf_op jit(solution)/shard_map/all_to_all | solution.py:72
  248.9 5.9 %reshape.235 = bf16[768,1,768]{2,1,0:T(2,128)(2,1)} reshape(bf16[8,2,36864]{2,1,0:T(2,128)(2,1)} %all_to_all.71) | data formatting | bytes 2359296
  254.9 2.9 copy.52
  257.7 2.9 copy.47
  260.6 4.6 %all-to-all-start.4 = ((bf16[8,768,96]{2,0,1:T(8,128)(2,1)}), bf16[8,768,96]{2,0,1:T(8,128)(2,1)}, u32[]{:S(2)}, u32[]{:S(2)}) async-start(bf16[8,768,96]{2,0,1:T(8,128)(2,1)} %copy.47), calls=%async_computation.4 | async-start | bytes 3145728 | tf_op jit(solution)/shard_map/all_to_all | solution.py:71
  266.7 3.5 %fusion.3 = f32[4608,128]{1,0:T(8,128)} fusion(bf16[4608,128]{1,0:T(8,128)(2,1)} %copy-done.1, bf16[128,640]{1,0:T(8,128)(2,1)S(1)} %bitcast.99), kind=kOutput, calls=%fused_computation.6 | convolution fusion | flops 152764416 | bytes 3571712 | tf_op jit(solution)/shard_map/dot_general | solution.py:59
  270.2 30.6 %all-to-all-done.4 = bf16[8,768,96]{2,0,1:T(8,128)(2,1)} async-done(((bf16[8,768,96]{2,0,1:T(8,128)(2,1)}), bf16[8,768,96]{2,0,1:T(8,128)(2,1)}, u32[]{:S(2)}, u32[]{:S(2)}) %all-to-all-start.4) | async-done | bytes 1179680 | tf_op jit(solution)/shard_map/all_to_all | solution.py:71
  300.7 1.6 copy.48
  305.2 3.9 %convert_element_type.76 = bf16[128,4608]{1,0:T(8,128)(2,1)} reshape(bf16[16,8,48,96]{3,2,1,0:T(8,128)(2,1)} %copy.50) | data formatting | bytes 2359296 | tf_op jit(solution)/shard_map/convert_element_type | solution.py:82
  309.1 3.6 %fusion.4 = bf16[4608,128]{1,0:T(8,128)(2,1)} fusion(f32[4608,128]{1,0:T(8,128)S(1)} %bitcast.84, f32[4608,128]{1,0:T(8,128)} %fusion.3, bf16[128,4608]{1,0:T(8,128)(2,1)} %convert_element_type.76, bf16[1,128,128]{2,1,0:T(8,128)(2,1)S(1)} %copy-done), kind=kOutput, calls=%fused_computation.7 | convolution fusion | flops 152764416 | bytes 7110656 | tf_op jit(solution)/shard_map/dot_general | solution.py:86
  (37 shorter events, 9.5 us)
Async XLA Ops:
  0.0 309.1 %copy-start = (bf16[1,128,128]{2,1,0:T(8,128)(2,1)S(1)}, bf16[1,128,128]{2,1,0:T(8,128)(2,1)}, u32[]{:S(2)}) copy-start(bf16[1,128,128]{2,1,0:T(8,128)(2,1)} %param.11) | copy-start | bytes 98308
  0.0 28.7 %collective-permute-start = (bf16[1,6,768,128]{3,2,1,0:T(8,128)(2,1)}, bf16[1,6,768,128]{3,2,1,0:T(8,128)(2,1)S(1)}, u32[]{:S(2)}, u32[]{:S(2)}) collective-permute-start(bf16[1,6,768,128]{3,2,1,0:T(8,128)(2,1)} %param.6), channel_id=1, source_target_pairs={{0,128},{128,0},{1,129},{129,1},{2,130},{130,2},{3,131},{131,3},{4... | collective-permute-start | bytes 3538952 | tf_op jit(solution)/shard_map/ppermute | solution.py:11
  28.7 8.5 %copy-start.4 = (s32[1,768]{1,0:T(1,128)S(1)}, s32[1,768]{1,0:T(1,128)}, u32[]{:S(2)}) copy-start(s32[1,768]{1,0:T(1,128)} %param.7) | copy-start | bytes 9220
  30.7 27.2 %all-to-all-start = ((bf16[6,768,128]{2,0,1:T(8,128)(2,1)}), bf16[6,768,128]{2,0,1:T(8,128)(2,1)S(1)}, u32[]{:S(2)}, u32[]{:S(2)}) async-start(bf16[6,768,128]{2,0,1:T(8,128)(2,1)} %copy.38), calls=%async_computation | async-start | bytes 3145728 | tf_op jit(solution)/shard_map/all_to_all | solution.py:49
  37.2 4.3 %collective-permute-start.1 = (bf16[1,768]{1,0:T(2,128)(2,1)S(1)}, bf16[1,768]{1,0:T(2,128)(2,1)S(1)}, u32[]{:S(2)}, u32[]{:S(2)}) collective-permute-start(bf16[1,768]{1,0:T(2,128)(2,1)S(1)} %convert_element_type.68), channel_id=1, source_target_pairs={{0,128},{128,0},{1,129},{129,1},{2,130},{130,2},{3,131},{131,3},{4... | collective-permute-start | bytes 4616 | tf_op jit(solution)/shard_map/ppermute | solution.py:11
  57.9 1.2 copy-start.2
  59.1 4.2 %copy-start.5 = (f32[1,128]{1,0:T(1,128)S(1)}, f32[1,128]{1,0:T(1,128)}, u32[]{:S(2)}) copy-start(f32[1,128]{1,0:T(1,128)} %param.9) | copy-start | bytes 1540
  63.1 3.7 %copy-start.3 = (bf16[1,128,640]{2,1,0:T(8,128)(2,1)S(1)}, bf16[1,128,640]{2,1,0:T(8,128)(2,1)}, u32[]{:S(2)}) copy-start(bf16[1,128,640]{2,1,0:T(8,128)(2,1)} %param.8) | copy-start | bytes 491524
  65.8 1.0 copy-start.1
  257.7 8.1 %copy-start.6 = (f32[1,128]{1,0:T(1,128)S(1)}, f32[1,128]{1,0:T(1,128)}, u32[]{:S(2)}) copy-start(f32[1,128]{1,0:T(1,128)} %param.10) | copy-start | bytes 1540
  260.6 40.1 %all-to-all-start.4 = ((bf16[8,768,96]{2,0,1:T(8,128)(2,1)}), bf16[8,768,96]{2,0,1:T(8,128)(2,1)}, u32[]{:S(2)}, u32[]{:S(2)}) async-start(bf16[8,768,96]{2,0,1:T(8,128)(2,1)} %copy.47), calls=%async_computation.4 | async-start | bytes 3145728 | tf_op jit(solution)/shard_map/all_to_all | solution.py:71
where the time goes:
time: 317 us; the launch traced here: 313 us
  blocking collectives  138 us (44%)
  waiting for transfers between devices  73 us (23%)
  local copies, waits for them, and re-layouts  47 us (15%)
  other arithmetic  25.8 us (8%)
  starting transfers between devices  17.9 us (6%)
  matrix products  10.5 us (3%)
    all_to_all x1, blocking collectives, local(): lax.all_to_all(stacked, 'row', split_axis=1, concat_axis=2, tiled=True)  81 us
    all_to_all x1, blocking collectives, local(): lax.all_to_all(lax.all_to_all(stacked, 'row', split_axis=1, concat_axis=2...  35.3 us
    all_to_all x1, waiting for transfers between devices, local(): lax.all_to_all(lax.all_to_all(channel_products(owned), 'col', split_axis=...  30.6 us
    ppermute x2, waiting for transfers between devices, from_behind(): lax.ppermute(shard, axis, [(i, (i + by) % size) for i in range(size)])  26.3 us
    all_to_all x1, blocking collectives, local(): lax.all_to_all(channel_products(owned), 'col', split_axis=2, concat_axis=...  21.9 us
    all_to_all x1, waiting for transfers between devices, local(): lax.all_to_all(arrived, 'col', split_axis=1, concat_axis=0, tiled=True)  16.1 us
    unnamed x19, local copies, waits for them, and re-layouts  14.3 us
    unnamed x2, other arithmetic  10.5 us
  transfers between devices with their start and end apart: 4, of which 4 were waited for; matrix products, arithmetic and copies ran while one was open for 2% of the time, Pallas kernels for 0%

commit v1 on v0

v1 whole, which is shorter than its diff:
```python
import functools

import jax
import jax.numpy as jnp
from jax import lax
from jax.experimental import pallas as pl
from jax.experimental.pallas import tpu as pltpu
from jax.sharding import PartitionSpec as P

EPS = 1e-05
MESH = pl.DeviceIdType.MESH


def from_behind(shard, axis, by):
    size = lax.axis_size(axis)
    return lax.ppermute(shard, axis, [(i, (i + by) % size) for i in range(size)])


def norm_rows(values, gain):
    center = jnp.mean(values, axis=-1, keepdims=True)
    deviate = values - center
    spread = jnp.mean(deviate * deviate, axis=-1, keepdims=True)
    return deviate * lax.rsqrt(spread + EPS) * gain


def exchange_kernel(n_row, n_col, x_ref, o_ref, send_sem, recv_sem):
    section = lax.axis_index("section")
    me = lax.axis_index("row") * n_col + lax.axis_index("col")
    total = n_row * n_col

    def device(d):
        t = lax.rem(me + d, total)
        return t, (section, t // n_col, lax.rem(t, n_col))

    barrier = pltpu.get_barrier_semaphore()

    def greet(d, carry):
        pl.semaphore_signal(barrier, inc=1, device_id=device(d)[1], device_id_type=MESH)
        return carry

    lax.fori_loop(1, total, greet, 0)
    own = pltpu.make_async_copy(x_ref.at[me], o_ref.at[me], recv_sem)
    own.start()
    pl.semaphore_wait(barrier, total - 1)

    def send(d, carry):
        t, where = device(d)
        pltpu.make_async_remote_copy(
            src_ref=x_ref.at[t],
            dst_ref=o_ref.at[me],
            send_sem=send_sem,
            recv_sem=recv_sem,
            device_id=where,
            device_id_type=MESH,
        ).start()
        return carry

    lax.fori_loop(1, total, send, 0)
    pltpu.make_async_copy(o_ref, o_ref, recv_sem).wait()
    sent = x_ref.at[pl.ds(0, total - 1)]
    pltpu.make_async_copy(sent, sent, send_sem).wait()


def exchange(blocks, n_row, n_col, cid):
    return pl.pallas_call(
        functools.partial(exchange_kernel, n_row, n_col),
        out_shape=jax.ShapeDtypeStruct(blocks.shape, blocks.dtype),
        in_specs=[pl.BlockSpec(memory_space=pltpu.VMEM)],
        out_specs=pl.BlockSpec(memory_space=pltpu.VMEM),
        scratch_shapes=[pltpu.SemaphoreType.DMA, pltpu.SemaphoreType.DMA],
        compiler_params=pltpu.CompilerParams(
            collective_id=cid, has_side_effects=True, vmem_limit_bytes=40 * 2**20
        ),
    )(blocks)


def local(n_row, n_col, handed, residue_mask, input_weights, input_gain, product_gain, output_weights):
    arrived, present = from_behind((handed, residue_mask.astype(jnp.bfloat16)), "section", 1)
    arrived = arrived[0]
    present = present[0].astype(jnp.float32)
    weights = input_weights[0]
    last_weights = output_weights[0]
    first_gain = input_gain[0]
    second_gain = product_gain[0]
    hidden = last_weights.shape[0]
    rows, size, channels = arrived.shape
    me = lax.axis_index("row") * n_col + lax.axis_index("col")
    normed = norm_rows(arrived.astype(jnp.float32), first_gain).astype(jnp.bfloat16)
    projected = lax.dot_general(
        weights[:, : 4 * hidden], normed.reshape(-1, channels), (((0,), (1,)), ((), ())),
        preferred_element_type=jnp.float32,
    ).reshape(4, hidden, rows, size)
    flags = lax.dynamic_slice_in_dim(present, me * rows, rows, 0)
    pair_mask = flags[:, None] * present[None, :]
    left = (jax.nn.sigmoid(projected[0]) * projected[1] * pair_mask).astype(jnp.bfloat16)
    right = (jax.nn.sigmoid(projected[2]) * projected[3] * pair_mask).astype(jnp.bfloat16)
    stacked = jnp.stack([left, right], axis=1).reshape(hidden, -1, 128)
    owned = exchange(stacked, n_row, n_col, 1).reshape(hidden, 2, rows, size)
    lefts = owned[:, 0].reshape(size, size)
    rights = owned[:, 1].reshape(size, size)
    product = lax.dot_general(
        lefts, rights, (((1,), (1,)), ((), ())), preferred_element_type=jnp.float32
    ).astype(jnp.bfloat16)
    row_count = size // n_row
    col_count = size // n_col
    blocks = product.reshape(n_row, row_count, n_col, col_count).transpose(0, 2, 1, 3)
    grid = exchange(blocks.reshape(hidden, -1, 128), n_row, n_col, 2).reshape(hidden, row_count, col_count)

    blocked = lax.all_to_all(arrived, "col", split_axis=1, concat_axis=0, tiled=True)
    block_norm = (
        norm_rows(blocked.astype(jnp.float32), first_gain).astype(jnp.bfloat16).reshape(-1, channels)
    )
    gating = jnp.dot(block_norm, weights[:, 4 * hidden :], preferred_element_type=jnp.float32)
    widened = grid.astype(jnp.float32)
    center = jnp.mean(widened, axis=0, keepdims=True)
    deviate = widened - center
    spread = jnp.mean(deviate * deviate, axis=0, keepdims=True)
    prod_norm = (deviate * lax.rsqrt(spread + EPS) * second_gain[:, None, None]).astype(jnp.bfloat16)
    update = lax.dot_general(
        prod_norm.reshape(hidden, -1), last_weights, (((0,), (0,)), ((), ())),
        preferred_element_type=jnp.float32,
    )
    result = blocked.astype(jnp.float32).reshape(-1, channels) + jax.nn.sigmoid(gating) * update
    return result.astype(jnp.bfloat16).reshape(1, row_count, col_count, channels)


def solution(mesh):
    placed = (
        P("section", ("row", "col"), None, None),
        P("section", None),
        P("section", None, None),
        P("section", None),
        P("section", None),
        P("section", None, None),
    )
    return jax.shard_map(
        functools.partial(local, mesh.shape["row"], mesh.shape["col"]),
        mesh=mesh,
        in_specs=placed,
        out_specs=P("section", "row", "col", None),
        check_vma=False,
    )
```

time: 317 us -> 210 us (0.66); the launches traced: 313 us -> 209 us
  blocking collectives: 138 us -> 0 us
  Pallas kernels: 0 us -> 107 us
  waiting for transfers between devices: 73 us -> 40.1 us
  local copies, waits for them, and re-layouts: 47 us -> 30.5 us
  other arithmetic: 25.8 us -> 14.9 us
  starting transfers between devices: 17.9 us -> 9.04 us
  matrix products: 10.5 us -> 7.2 us
    all_to_all x3 -> x0, blocking collectives: 138 us -> none  [the longest x1 81 us: local(): lax.all_to_all(stacked, 'row', split_axis=1, concat_axis=2, tiled=True)]
    pallas_call x0 -> x2, Pallas kernels: none -> 107 us  [exchange(): pl.pallas_call(functools.partial(exchange_kernel, n_row, n_col), out_shap...]
    all_to_all x1 -> x0, waiting for transfers between devices: 30.6 us -> none  [local(): lax.all_to_all(lax.all_to_all(channel_products(owned), 'col', split_axis=...]
    all_to_all x5 -> x0, local copies, waits for them, and re-layouts: 11.6 us -> none  [the longest x2 6.97 us: local(): lax.all_to_all(stacked, 'row', split_axis=1, concat_axis=2, tiled=True)]
    reshape x0 -> x4, local copies, waits for them, and re-layouts: none -> 11.6 us  [the longest x2 4.57 us: local(): product.reshape(n_row, row_count, n_col, col_count).transpose(0, 2, 1, 3)]
    unnamed x19 -> x22, local copies, waits for them, and re-layouts: 14.3 us -> 3.38 us
    unnamed x2 -> x0, other arithmetic: 10.5 us -> none
    mul x4 -> x0, local copies, waits for them, and re-layouts: 7.05 us -> none  [the longest x1 3.45 us: factors(): right_factor = jax.nn.sigmoid(projected[2]) * projected[3] * pair_mask]
  transfers between devices with their start and end apart: 4 -> 3, of which waited for: 4 -> 2; matrix products, arithmetic and copies ran while one was open for 2% -> 3% of each run, Pallas kernels for 0% -> 0%
where the time goes in v1:
time: 210 us; the launch traced here: 209 us
  Pallas kernels  107 us (51%)
  waiting for transfers between devices  40.1 us (19%)
  local copies, waits for them, and re-layouts  30.5 us (15%)
  other arithmetic  14.9 us (7%)
  starting transfers between devices  9.04 us (4%)
  matrix products  7.2 us (3%)
    pallas_call x2, Pallas kernels, exchange(): pl.pallas_call(functools.partial(exchange_kernel, n_row, n_col), out_shap...  107 us
    ppermute x2, waiting for transfers between devices, from_behind(): lax.ppermute(shard, axis, [(i, (i + by) % size) for i in range(size)])  24.3 us
    all_to_all x1, waiting for transfers between devices, local(): lax.all_to_all(arrived, 'col', split_axis=1, concat_axis=0, tiled=True)  15.8 us
    all_to_all x1, starting transfers between devices, local(): lax.all_to_all(arrived, 'col', split_axis=1, concat_axis=0, tiled=True)  5.19 us
    reshape x2, local copies, waits for them, and re-layouts, local(): product.reshape(n_row, row_count, n_col, col_count).transpose(0, 2, 1, 3)  4.57 us
  transfers between devices with their start and end apart: 3, of which 2 were waited for; matrix products, arithmetic and copies ran while one was open for 3% of the time, Pallas kernels for 0%

profile of v1, /device:TPU:1, one launch (start us, length us, event | category | flops | bytes accessed | tf_op | source)
XLA Modules:
  0.0 209.0 jit_solution(16802120035043242736)
XLA Ops:
  0.0 3.8 %collective-permute-start = (bf16[1,6,768,128]{3,2,1,0:T(8,128)(2,1)}, bf16[1,6,768,128]{3,2,1,0:T(8,128)(2,1)S(1)}, u32[]{:S(2)}, u32[]{:S(2)}) collective-permute-start(bf16[1,6,768,128]{3,2,1,0:T(8,128)(2,1)} %param.6), channel_id=1, source_target_pairs={{0,128},{128,0},{1,129},{129,1},{2,130},{130,2},{3,131},{131,3},{4... | collective-permute-start | bytes 3538952 | tf_op jit(solution)/shard_map/ppermute | solution.py:16
  4.5 24.2 %collective-permute-done.1 = bf16[1,768]{1,0:T(2,128)(2,1)S(1)} collective-permute-done((bf16[1,768]{1,0:T(2,128)(2,1)S(1)}, bf16[1,768]{1,0:T(2,128)(2,1)S(1)}, u32[]{:S(2)}, u32[]{:S(2)}) %collective-permute-start.1) | collective-permute-done | bytes 1568 | tf_op jit(solution)/shard_map/ppermute | solution.py:16
  29.4 1.4 fusion.11
  30.9 1.4 convolution_bitcast_fusion
  32.3 1.2 slice_multiply_fusion.1
  33.5 0.8 multiply_convert_fusion.1
  34.4 1.6 pad_maximum_fusion
  36.0 3.2 %copy.56.x_ref = bf16[128,72,128]{2,1,0:T(8,128)(2,1)S(1)} copy(bf16[128,72,128]{0,2,1:T(8,128)(2,1)} %bitcast.58) | data formatting | bytes 4718592 | tf_op jit(solution)/shard_map/reshape | solution.py:97
  39.2 66.0 %shard_map.64 = bf16[128,72,128]{2,1,0:T(8,128)(2,1)S(1)} custom-call(bf16[128,72,128]{2,1,0:T(8,128)(2,1)S(1)} %copy.56.x_ref), custom_call_target="tpu_custom_call" | custom-call | tf_op jit(solution)/shard_map/pallas_call | solution.py:65
  105.2 1.4 copy-done.1
  106.6 3.3 %copy.57 = bf16[128,72,128]{0,2,1:T(8,128)(2,1)S(1)} copy(bf16[128,72,128]{2,1,0:T(8,128)(2,1)} %copy-done.1) | data formatting | bytes 4718592 | tf_op jit(solution)/shard_map/pallas_call | solution.py:65
  109.8 1.6 fusion.33
  111.4 2.2 %copy.58 = bf16[128,1,6,768]{3,2,0,1:T(8,128)(2,1)S(1)} copy(bf16[128,1,6,768]{0,3,2,1:T(8,128)(2,1)} %get-tuple-element.10) | data formatting | bytes 2359296 | tf_op jit(solution)/shard_map/slice | solution.py:99
  113.6 1.3 reshape_squeeze.6
  114.9 1.1 copy.59
  116.0 1.2 reshape_squeeze.7
  117.6 3.4 %convolution_convert_fusion = bf16[768,768]{1,0:T(8,128)(2,1)} fusion(bf16[768,768]{1,0:T(8,128)(2,1)S(1)} %copy-done.7, bf16[768,768]{1,0:T(8,128)(2,1)} %reshape_squeeze.7), kind=kOutput, calls=%fused_computation.45 | convolution fusion | flops 906559488 | bytes 3538944 | tf_op jit(solution)/shard_map/dot_general | solution.py:101
  121.0 3.1 %reshape.256 = bf16[16,48,8,96]{3,2,1,0:T(8,128)(2,1)S(1)} reshape(bf16[768,768]{1,0:T(8,128)(2,1)} %convolution_convert_fusion) | data formatting | bytes 2359296 | tf_op jit(solution)/shard_map/reshape | solution.py:106
  124.1 1.5 copy.66
  125.6 3.8 %reshape.257.x_ref = bf16[128,36,128]{2,1,0:T(8,128)(2,1)S(1)} reshape(bf16[16,8,48,96]{3,2,1,0:T(8,128)(2,1)} %bitcast.60) | data formatting | bytes 2359296 | tf_op jit(solution)/shard_map/reshape | solution.py:107
  129.4 41.1 %shard_map.65 = bf16[128,36,128]{2,1,0:T(8,128)(2,1)S(1)} custom-call(bf16[128,36,128]{2,1,0:T(8,128)(2,1)S(1)} %reshape.257.x_ref), custom_call_target="tpu_custom_call" | custom-call | tf_op jit(solution)/shard_map/pallas_call | solution.py:65
  170.5 2.0 copy.50
  172.5 5.2 %all-to-all-start = ((bf16[6,768,128]{2,0,1:T(8,128)(2,1)}), bf16[6,768,128]{2,0,1:T(8,128)(2,1)S(1)}, u32[]{:S(2)}, u32[]{:S(2)}) async-start(bf16[6,768,128]{2,0,1:T(8,128)(2,1)} %copy.50), calls=%async_computation | async-start | bytes 3145728 | tf_op jit(solution)/shard_map/all_to_all | solution.py:109
  178.4 1.5 fusion.9
  179.9 2.7 %copy.61 = bf16[128,36,128]{0,2,1:T(8,128)(2,1)} copy(bf16[128,36,128]{2,1,0:T(8,128)(2,1)} %fusion.9) | data formatting | bytes 2359296 | tf_op jit(solution)/shard_map/convert_element_type | solution.py:118
  182.6 15.8 %all-to-all-done = bf16[6,768,128]{2,0,1:T(8,128)(2,1)S(1)} async-done(((bf16[6,768,128]{2,0,1:T(8,128)(2,1)}), bf16[6,768,128]{2,0,1:T(8,128)(2,1)S(1)}, u32[]{:S(2)}, u32[]{:S(2)}) %all-to-all-start) | async-done | bytes 1179680 | tf_op jit(solution)/shard_map/all_to_all | solution.py:109
  198.4 1.2 copy-done.4
  199.6 2.3 %bitcast_reduce_fusion = (f32[8,6,96]{2,1,0:T(8,128)S(1)}, f32[6,8,96,128]{3,2,0,1:T(8,128)S(1)}) fusion(bf16[6,8,96,128]{3,0,2,1:T(8,128)(2,1)} %bitcast.59), kind=kLoop, calls=%fused_computation.38 | loop fusion | flops 585216 | bytes 3557376 | tf_op jit(solution)/shard_map/reduce_sum | solution.py:20
  201.9 1.6 fusion.25
  203.7 2.5 %fusion.23 = bf16[4608,128]{1,0:T(8,128)(2,1)S(1)} fusion(f32[6,8,96,128]{3,2,0,1:T(8,128)S(1)} %get-tuple-element.6, f32[128]{0:T(128)S(1)} %bitcast.65, f32[4608]{0:T(1024)S(1)} %rsqrt.31, f32[4608]{0:T(1024)S(1)} %div.52), kind=kLoop, calls=%fused_computation.37 | loop fusion | flops 2359296 | bytes 3576320 | tf_op jit(solution)/shard_map/convert_element_type | solution.py:111
  206.2 0.8 fusion.3
  207.5 1.6 fusion.4
  (40 shorter events, 2.9 us)
Async XLA Ops:
  0.0 207.0 %copy-start = (bf16[1,128,128]{2,1,0:T(8,128)(2,1)S(1)}, bf16[1,128,128]{2,1,0:T(8,128)(2,1)}, u32[]{:S(2)}) copy-start(bf16[1,128,128]{2,1,0:T(8,128)(2,1)} %param.11) | copy-start | bytes 98308
  0.0 30.8 %copy-start.9 = (f32[1,128]{1,0:T(1,128)S(1)}, f32[1,128]{1,0:T(1,128)}, u32[]{:S(2)}) copy-start(f32[1,128]{1,0:T(1,128)} %param.9) | copy-start | bytes 1540
  0.0 30.8 %copy-start.8 = (bf16[1,128,640]{2,1,0:T(8,128)(2,1)S(1)}, bf16[1,128,640]{2,1,0:T(8,128)(2,1)}, u32[]{:S(2)}) copy-start(bf16[1,128,640]{2,1,0:T(8,128)(2,1)} %param.8) | copy-start | bytes 491524
  0.0 29.0 %collective-permute-start = (bf16[1,6,768,128]{3,2,1,0:T(8,128)(2,1)}, bf16[1,6,768,128]{3,2,1,0:T(8,128)(2,1)S(1)}, u32[]{:S(2)}, u32[]{:S(2)}) collective-permute-start(bf16[1,6,768,128]{3,2,1,0:T(8,128)(2,1)} %param.6), channel_id=1, source_target_pairs={{0,128},{128,0},{1,129},{129,1},{2,130},{130,2},{3,131},{131,3},{4... | collective-permute-start | bytes 3538952 | tf_op jit(solution)/shard_map/ppermute | solution.py:16
  4.5 24.3 %collective-permute-start.1 = (bf16[1,768]{1,0:T(2,128)(2,1)S(1)}, bf16[1,768]{1,0:T(2,128)(2,1)S(1)}, u32[]{:S(2)}, u32[]{:S(2)}) collective-permute-start(bf16[1,768]{1,0:T(2,128)(2,1)S(1)} %convert_element_type.100), channel_id=1, source_target_pairs={{0,128},{128,0},{1,129},{129,1},{2,130},{130,2},{3,131},{131,3},{4... | collective-permute-start | bytes 4616 | tf_op jit(solution)/shard_map/ppermute | solution.py:16
  29.0 3.3 %copy-start.2 = (bf16[1,6,768,128]{3,2,1,0:T(8,128)(2,1)}, bf16[1,6,768,128]{3,2,1,0:T(8,128)(2,1)S(1)}, u32[]{:S(2)}) copy-start(bf16[1,6,768,128]{3,2,1,0:T(8,128)(2,1)S(1)} %collective-permute-done) | copy-start | bytes 3538948
  105.1 1.4 copy-start.1
  111.4 3.5 %copy-start.6 = (bf16[128,1,6,768]{0,3,2,1:T(8,128)(2,1)S(1)}, bf16[128,1,6,768]{0,3,2,1:T(8,128)(2,1)}, u32[]{:S(2)}) copy-start(bf16[128,1,6,768]{0,3,2,1:T(8,128)(2,1)} %get-tuple-element.9) | copy-start | bytes 3538948
  116.0 1.6 copy-start.7
  129.4 41.1 %copy-start.3 = (bf16[1,6,768,128]{3,2,1,0:T(8,128)(2,1)S(1)}, bf16[1,6,768,128]{3,2,1,0:T(8,128)(2,1)}, u32[]{:S(2)}) copy-start(bf16[1,6,768,128]{3,2,1,0:T(8,128)(2,1)} %copy-done.2) | copy-start | bytes 3538948
  172.5 5.9 %copy-start.10 = (f32[1,128]{1,0:T(1,128)S(1)}, f32[1,128]{1,0:T(1,128)}, u32[]{:S(2)}) copy-start(f32[1,128]{1,0:T(1,128)} %param.10) | copy-start | bytes 1540
  172.5 25.9 %all-to-all-start = ((bf16[6,768,128]{2,0,1:T(8,128)(2,1)}), bf16[6,768,128]{2,0,1:T(8,128)(2,1)S(1)}, u32[]{:S(2)}, u32[]{:S(2)}) async-start(bf16[6,768,128]{2,0,1:T(8,128)(2,1)} %copy.50), calls=%async_computation | async-start | bytes 3145728 | tf_op jit(solution)/shard_map/all_to_all | solution.py:109
  198.4 1.2 copy-start.4
  206.2 1.3 copy-start.5

commit v2 on v0

v2 whole, which is shorter than its diff:
```python
import functools

import jax
import jax.numpy as jnp
from jax import lax
from jax.experimental import pallas as pl
from jax.experimental.pallas import tpu as pltpu
from jax.sharding import PartitionSpec as P

EPS = 1e-05
LANES = 128
MESH = pl.DeviceIdType.MESH
BF16 = jnp.bfloat16
F32 = jnp.float32


def norm(values, gain, axis):
    center = jnp.mean(values, axis=axis, keepdims=True)
    deviate = values - center
    spread = jnp.mean(deviate * deviate, axis=axis, keepdims=True)
    return (deviate * lax.rsqrt(spread + EPS) * gain).astype(BF16)


def wait_for(ref, sem):
    pltpu.make_async_copy(ref, ref, sem).wait()


def kernel(
    n_row, n_col,
    handed, mask, w_in, g_in, g_prod, w_out, out,
    slab, flags, w_cols, g_cols, factor_f32, factor_out, factors, products,
    packed_f32, product_out, product_in, product_f32, block, gate,
    flag_sems, slab_send, slab_recv, factor_send, factor_recv,
    product_send, product_recv, block_send, block_recv,
):
    rows, size, channels = slab.shape
    hidden = w_out.shape[1]
    k_tiles = size // LANES
    devices = n_row * n_col
    row_count, col_count = size // n_row, size // n_col
    parts, _, part_rows = product_out.shape[0], 0, 2 * product_out.shape[2]
    section, row, col = (lax.axis_index(a) for a in ("section", "row", "col"))
    me = row * n_col + col
    partner = (1 - section, row, col)

    def at(t):
        return (section, t // n_col, lax.rem(t, n_col))

    barrier = pltpu.get_barrier_semaphore()
    pl.semaphore_signal(barrier, inc=1, device_id=partner, device_id_type=MESH)

    def greet(d, carry):
        pl.semaphore_signal(barrier, inc=1, device_id=at(lax.rem(me + d, devices)), device_id_type=MESH)
        return carry

    lax.fori_loop(1, devices, greet, 0)
    w_cols[...] = w_in[0].astype(F32).T.astype(BF16)
    g_cols[...] = jnp.broadcast_to(g_prod[...], (LANES, hidden)).T
    pl.semaphore_wait(barrier, devices)

    flag_copy = pltpu.make_async_remote_copy(
        src_ref=mask, dst_ref=flags, send_sem=flag_sems.at[0], recv_sem=flag_sems.at[1],
        device_id=partner, device_id_type=MESH,
    )
    flag_copy.start()

    def tile(kt):
        return pl.ds(pl.multiple_of(kt * LANES, LANES), LANES)

    def slab_copy(kt):
        return pltpu.make_async_remote_copy(
            src_ref=handed.at[0, :, tile(kt)], dst_ref=slab.at[:, tile(kt)],
            send_sem=slab_send, recv_sem=slab_recv.at[kt],
            device_id=partner, device_id_type=MESH,
        )

    slab_copy(0).start()
    slab_copy(1).start()
    flag_copy.wait()

    per_owner = 2 * rows
    factor_rows = factor_out.reshape(k_tiles * devices * per_owner, LANES)
    all_flags = flags[...].astype(F32)
    places = lax.broadcasted_iota(jnp.int32, all_flags.shape, 1)
    own_flags = [
        jnp.sum(jnp.where(places == me * rows + i, all_flags, 0.0), axis=1, keepdims=True)
        for i in range(rows)
    ]

    def factor_step(kt, carry):
        wait_for(slab.at[:, tile(kt)], slab_recv.at[kt])

        @pl.when(kt + 2 < k_tiles)
        def _():
            slab_copy(kt + 2).start()

        k_flags = flags[:, tile(kt)].astype(F32)
        for i in range(rows):
            normed = norm(slab[i, tile(kt), :].astype(F32), g_in[...], 1)
            projected = lax.dot_general(
                w_cols[: 4 * hidden], normed, (((1,), (1,)), ((), ())), preferred_element_type=F32
            )
            pair_flags = k_flags * own_flags[i]
            for side in range(2):
                gates = projected[2 * side * hidden : (2 * side + 1) * hidden]
                values = projected[(2 * side + 1) * hidden : (2 * side + 2) * hidden]
                factor_f32[pl.ds(side * rows + i, hidden, stride=per_owner), :] = (
                    jax.nn.sigmoid(gates) * values * pair_flags
                )
        begin = pl.multiple_of(kt * (devices * per_owner), devices * per_owner)
        factor_rows[pl.ds(begin, devices * per_owner), :] = factor_f32[...].astype(BF16)
        target = factors.at[:, kt, pl.ds(me * (rows // 2), rows // 2)]
        pltpu.make_async_copy(factor_out.at[kt, me], target, factor_recv.at[kt]).start()

        def send(d, c):
            t = lax.rem(me + d, devices)
            pltpu.make_async_remote_copy(
                src_ref=factor_out.at[kt, t], dst_ref=target,
                send_sem=factor_send, recv_sem=factor_recv.at[kt],
                device_id=at(t), device_id_type=MESH,
            ).start()
            return c

        lax.fori_loop(1, devices, send, 0)
        return carry

    lax.fori_loop(0, k_tiles, factor_step, 0)

    def columns(c):
        return pl.ds(pl.multiple_of(c * col_count, col_count), col_count)

    block_rows = block.at[pl.ds(col * rows, rows)]
    pltpu.make_async_copy(slab.at[:, columns(col)], block_rows, block_recv).start()

    def send_block(d, carry):
        c = lax.rem(col + d, n_col)
        pltpu.make_async_remote_copy(
            src_ref=slab.at[:, columns(c)], dst_ref=block_rows,
            send_sem=block_send, recv_sem=block_recv,
            device_id=(section, row, c), device_id_type=MESH,
        ).start()
        return carry

    lax.fori_loop(1, n_col, send_block, 0)

    arrived = factors.reshape(2 * k_tiles * size, LANES)
    strip = 256

    def product_step(first, kt, carry):
        wait_for(factors.at[:, kt], factor_recv.at[kt])
        right = arrived[pl.ds(pl.multiple_of((k_tiles + kt) * size, size), size), :]
        for m in range(0, size, strip):
            left = arrived[pl.ds(pl.multiple_of(kt * size + m, strip), strip), :]
            part = lax.dot_general(left, right, (((1,), (1,)), ((), ())), preferred_element_type=F32)
            products[m : m + strip, :] = part if first else products[m : m + strip, :] + part
        return carry

    product_step(True, 0, 0)
    lax.fori_loop(1, 3, functools.partial(product_step, False), 0)

    wait_for(block, block_recv)

    def gate_step(i, carry):
        normed = norm(block[i].astype(F32), g_in[...], 1)
        gate[i] = jax.nn.sigmoid(
            jnp.dot(normed, w_in[0, :, 4 * hidden :], preferred_element_type=F32)
        )
        return carry

    lax.fori_loop(0, row_count, gate_step, 0)
    lax.fori_loop(3, k_tiles, functools.partial(product_step, False), 0)

    kept = parts * part_rows
    product_rows = product_out.reshape(parts * devices * part_rows, LANES)
    spare = LANES - col_count

    for part in range(parts):

        def pack(d, carry, part=part):
            r = lax.rem(row + d, n_row)
            tile_rows = products[pl.ds(pl.multiple_of(r * row_count, row_count), row_count), :]
            for c in range(n_col):
                into = slice(c * part_rows, (c + 1) * part_rows)
                packed_f32[into, :col_count] = tile_rows[
                    part * part_rows : (part + 1) * part_rows, c * col_count : (c + 1) * col_count
                ]
                begin = c * col_count + part * spare
                packed_f32[into, col_count:] = tile_rows[kept:, begin : begin + spare]
            base = part * devices + r * n_col
            product_rows[pl.ds(pl.multiple_of(base * part_rows, n_col * part_rows), n_col * part_rows), :] = (
                packed_f32[...].astype(BF16)
            )

            def send(e, cc):
                c = lax.rem(col + e, n_col)
                t = r * n_col + c

                @pl.when(t != me)
                def _():
                    pltpu.make_async_remote_copy(
                        src_ref=product_out.at[part, t], dst_ref=product_in.at[part, me],
                        send_sem=product_send, recv_sem=product_recv.at[part],
                        device_id=(section, r, c), device_id_type=MESH,
                    ).start()

                @pl.when(t == me)
                def _():
                    pltpu.make_async_copy(
                        product_out.at[part, me], product_in.at[part, me], product_recv.at[part]
                    ).start()

                return cc

            lax.fori_loop(0, n_col, send, 0)
            return carry

        lax.fori_loop(0, n_row, pack, 0)

    product_in_rows = product_in.reshape(parts * devices * part_rows, LANES)
    for part in range(parts):
        wait_for(product_in.at[part], product_recv.at[part])
        product_f32[...] = product_in_rows[
            part * devices * part_rows : (part + 1) * devices * part_rows, :
        ].astype(F32)

        def finish(q, carry, part=part):
            normed = norm(product_f32[pl.ds(q, devices, stride=part_rows), :], g_cols[...], 0)
            update = lax.dot_general(
                normed, w_out[0], (((0,), (0,)), ((), ())), preferred_element_type=F32
            )
            i = part * part_rows + q
            out[0, i] = (block[i].astype(F32) + gate[i] * update[:col_count]).astype(BF16)
            i, j = kept + q, slice(part * spare, (part + 1) * spare)
            out[0, i, j] = (block[i, j].astype(F32) + gate[i, j] * update[col_count:]).astype(BF16)
            return carry

        lax.fori_loop(0, part_rows, finish, 0)

    wait_for(slab, slab_send)
    wait_for(factor_out.at[:, pl.ds(0, devices - 1)], factor_send)
    wait_for(product_out.at[:, pl.ds(0, devices - 1)], product_send)
    wait_for(block.at[pl.ds(0, (n_col - 1) * rows)], block_send)


def local(n_row, n_col, handed, residue_mask, input_weights, input_gain, product_gain, output_weights):
    _, rows, size, channels = handed.shape
    hidden = output_weights.shape[1]
    devices = n_row * n_col
    k_tiles = size // LANES
    row_count, col_count = size // n_row, size // n_col
    message = row_count * col_count // LANES
    parts = 3
    part_rows = message // parts
    vmem = pl.BlockSpec(memory_space=pltpu.VMEM)
    dma = pltpu.SemaphoreType.DMA
    return pl.pallas_call(
        functools.partial(kernel, n_row, n_col),
        out_shape=jax.ShapeDtypeStruct((1, row_count, col_count, channels), BF16),
        in_specs=[pl.BlockSpec(memory_space=pl.ANY)] + [vmem] * 5,
        out_specs=vmem,
        scratch_shapes=[
            pltpu.VMEM((rows, size, channels), BF16),
            pltpu.VMEM((1, size), jnp.int32),
            pltpu.VMEM(input_weights.shape[:0:-1], BF16),
            pltpu.VMEM((hidden, LANES), F32),
            pltpu.VMEM((devices * 2 * rows, LANES), F32),
            pltpu.VMEM((k_tiles, devices, 2, rows // 2, 2, LANES), BF16),
            pltpu.VMEM((2, k_tiles, size // 2, 2, LANES), BF16),
            pltpu.VMEM((size, size), F32),
            pltpu.VMEM((n_col * part_rows, LANES), F32),
            pltpu.VMEM((parts, devices, part_rows // 2, 2, LANES), BF16),
            pltpu.VMEM((parts, devices, part_rows // 2, 2, LANES), BF16),
            pltpu.VMEM((devices * part_rows, LANES), F32),
            pltpu.VMEM((row_count, col_count, channels), BF16),
            pltpu.VMEM((row_count, col_count, channels), F32),
            dma((2,)), dma, dma((k_tiles,)), dma, dma((k_tiles,)),
            dma, dma((parts,)), dma, dma,
        ],
        compiler_params=pltpu.CompilerParams(
            collective_id=0, has_side_effects=True, vmem_limit_bytes=48 * 2**20
        ),
    )(handed, residue_mask, input_weights, input_gain, product_gain, output_weights)


def solution(mesh):
    placed = (
        P("section", ("row", "col"), None, None),
        P("section", None),
        P("section", None, None),
        P("section", None),
        P("section", None),
        P("section", None, None),
    )
    return jax.shard_map(
        functools.partial(local, mesh.shape["row"], mesh.shape["col"]),
        mesh=mesh,
        in_specs=placed,
        out_specs=P("section", "row", "col", None),
        check_vma=False,
    )
```

time: 317 us -> 138 us (0.44); the launches traced: 313 us -> 137 us
  blocking collectives: 138 us -> 0 us
  Pallas kernels: 0 us -> 131 us
  waiting for transfers between devices: 73 us -> 0 us
  local copies, waits for them, and re-layouts: 47 us -> 5.95 us
  other arithmetic: 25.8 us -> 0 us
  starting transfers between devices: 17.9 us -> 0 us
  matrix products: 10.5 us -> 0 us
    all_to_all x3 -> x0, blocking collectives: 138 us -> none  [the longest x1 81 us: local(): lax.all_to_all(stacked, 'row', split_axis=1, concat_axis=2, tiled=True)]
    pallas_call x0 -> x1, Pallas kernels: none -> 131 us  [local(): pl.pallas_call(functools.partial(kernel, n_row, n_col), out_shape=jax.Sha...]
    all_to_all x2 -> x0, waiting for transfers between devices: 46.7 us -> none  [the longest x1 30.6 us: local(): lax.all_to_all(lax.all_to_all(channel_products(owned), 'col', split_axis=...]
    ppermute x2 -> x0, waiting for transfers between devices: 26.3 us -> none  [from_behind(): lax.ppermute(shard, axis, [(i, (i + by) % size) for i in range(size)])]
    convert_element_type x3 -> x0, local copies, waits for them, and re-layouts: 11.8 us -> none  [the longest x1 6.61 us: channel_products(): return jnp.einsum('hik,hjk->hij', owned[0], owned[1], preferred_element_t...]
    all_to_all x5 -> x0, local copies, waits for them, and re-layouts: 11.6 us -> none  [the longest x2 6.97 us: local(): lax.all_to_all(stacked, 'row', split_axis=1, concat_axis=2, tiled=True)]
    all_to_all x2 -> x0, starting transfers between devices: 11.1 us -> none  [the longest x1 6.53 us: local(): lax.all_to_all(arrived, 'col', split_axis=1, concat_axis=0, tiled=True)]
    dot_general x4 -> x0, matrix products: 10.5 us -> none  [the longest x1 3.55 us: local(): lax.dot_general(prod_norm, last_weights, (((0,), (0,)), ((), ())), prefer...]
  transfers between devices with their start and end apart: 4 -> 0, of which waited for: 4 -> 0; matrix products, arithmetic and copies ran while one was open for 2% -> 0% of each run, Pallas kernels for 0% -> 0%
where the time goes in v2:
time: 138 us; the launch traced here: 137 us
  Pallas kernels  131 us (95%)
  local copies, waits for them, and re-layouts  5.95 us (4%)
    pallas_call x1, Pallas kernels, local(): pl.pallas_call(functools.partial(kernel, n_row, n_col), out_shape=jax.Sha...  131 us
    unnamed x13, local copies, waits for them, and re-layouts  5.95 us

profile of v2, /device:TPU:1, one launch (start us, length us, event | category | flops | bytes accessed | tf_op | source)
XLA Modules:
  0.0 137.3 jit_solution(2896703444983642553)
XLA Ops:
  0.0 0.0 copy-start
  0.0 1.3 copy-done
  1.3 0.0 copy-start.1
  1.3 0.9 copy-done.1
  2.2 0.0 copy-start.2
  2.2 0.8 copy-done.2
  2.9 0.0 copy-start.3
  2.9 0.7 copy-done.3
  3.6 0.0 copy-start.4
  3.6 0.7 copy-done.4
  4.3 0.0 copy-start.5
  4.3 0.7 copy-done.5
  4.9 131.3 %shard_map.64 = bf16[1,48,96,128]{3,2,1,0:T(8,128)(2,1)S(1)} custom-call(bf16[1,6,768,128]{3,2,1,0:T(8,128)(2,1)S(1)} %copy-done, s32[1,768]{1,0:T(1,128)S(1)} %copy-done.3, bf16[1,128,640]{2,1,0:T(8,128)(2,1)S(1)} %copy-done.1, f32[1,128]{1,0:T(1,128)S(1)} %copy-done.4, f32[1,128]{1,0:T(1,128)S(1)} %copy-done.5, bf16[1,128,128]{2,1,0:T(8,128)(2,1)S(1)} %copy-done.2), custom_call_target="tpu_custom_call" | custom-call | tf_op jit(solution)/shard_map/pallas_call | solution.py:256
  136.3 1.0 copy.8
Async XLA Ops:
  0.0 1.3 copy-start
  1.3 0.9 copy-start.1
  2.2 0.8 copy-start.2
  2.9 0.7 copy-start.3
  3.6 0.7 copy-start.4
  4.3 0.7 copy-start.5

commit v3 on v2

--- a/solution.py
+++ b/solution.py
@@ -27,10 +27,10 @@
 
 def kernel(
     n_row, n_col,
-    handed, mask, w_in, g_in, g_prod, w_out, out,
-    slab, flags, w_cols, g_cols, factor_f32, factor_out, factors, products,
+    handed, mask, w_in_hbm, g_in_hbm, g_prod_hbm, w_out_hbm, out,
+    w_in, g_in, g_prod, w_out, slab, flags, w_cols, g_cols, factor_f32, factor_out, factors, products,
     packed_f32, product_out, product_in, product_f32, block, gate,
-    flag_sems, slab_send, slab_recv, factor_send, factor_recv,
+    load_sems, flag_sems, slab_send, slab_recv, factor_send, factor_recv,
     product_send, product_recv, block_send, block_recv,
 ):
     rows, size, channels = slab.shape
@@ -46,6 +46,14 @@
     def at(t):
         return (section, t // n_col, lax.rem(t, n_col))
 
+    loads = [
+        pltpu.make_async_copy(source, target, load_sems.at[i])
+        for i, (source, target) in enumerate(
+            ((w_in_hbm, w_in), (g_prod_hbm, g_prod), (g_in_hbm, g_in), (w_out_hbm, w_out))
+        )
+    ]
+    for load in loads:
+        load.start()
     barrier = pltpu.get_barrier_semaphore()
     pl.semaphore_signal(barrier, inc=1, device_id=partner, device_id_type=MESH)
 
@@ -54,6 +62,8 @@
         return carry
 
     lax.fori_loop(1, devices, greet, 0)
+    for load in loads:
+        load.wait()
     w_cols[...] = w_in[0].astype(F32).T.astype(BF16)
     g_cols[...] = jnp.broadcast_to(g_prod[...], (LANES, hidden)).T
     pl.semaphore_wait(barrier, devices)
@@ -77,6 +87,26 @@
     slab_copy(0).start()
     slab_copy(1).start()
     flag_copy.wait()
+
+    def columns(c):
+        return pl.ds(pl.multiple_of(c * col_count, col_count), col_count)
+
+    block_rows = block.at[pl.ds(col * rows, rows)]
+
+    def send_block(c, carry):
+        @pl.when(c != col)
+        def _():
+            pltpu.make_async_remote_copy(
+                src_ref=slab.at[:, columns(c)], dst_ref=block_rows,
+                send_sem=block_send, recv_sem=block_recv,
+                device_id=(section, row, c), device_id_type=MESH,
+            ).start()
+
+        @pl.when(c == col)
+        def _():
+            pltpu.make_async_copy(slab.at[:, columns(c)], block_rows, block_recv).start()
+
+        return carry
 
     per_owner = 2 * rows
     factor_rows = factor_out.reshape(k_tiles * devices * per_owner, LANES)
@@ -126,22 +156,10 @@
 
     lax.fori_loop(0, k_tiles, factor_step, 0)
 
-    def columns(c):
-        return pl.ds(pl.multiple_of(c * col_count, col_count), col_count)
-
-    block_rows = block.at[pl.ds(col * rows, rows)]
-    pltpu.make_async_copy(slab.at[:, columns(col)], block_rows, block_recv).start()
-
-    def send_block(d, carry):
-        c = lax.rem(col + d, n_col)
-        pltpu.make_async_remote_copy(
-            src_ref=slab.at[:, columns(c)], dst_ref=block_rows,
-            send_sem=block_send, recv_sem=block_recv,
-            device_id=(section, row, c), device_id_type=MESH,
-        ).start()
-        return carry
-
-    lax.fori_loop(1, n_col, send_block, 0)
+    def send_block_turn(d, carry):
+        return send_block(lax.rem(col + d, n_col), carry)
+
+    lax.fori_loop(0, n_col, send_block_turn, 0)
 
     arrived = factors.reshape(2 * k_tiles * size, LANES)
     strip = 256
@@ -156,19 +174,7 @@
         return carry
 
     product_step(True, 0, 0)
-    lax.fori_loop(1, 3, functools.partial(product_step, False), 0)
-
-    wait_for(block, block_recv)
-
-    def gate_step(i, carry):
-        normed = norm(block[i].astype(F32), g_in[...], 1)
-        gate[i] = jax.nn.sigmoid(
-            jnp.dot(normed, w_in[0, :, 4 * hidden :], preferred_element_type=F32)
-        )
-        return carry
-
-    lax.fori_loop(0, row_count, gate_step, 0)
-    lax.fori_loop(3, k_tiles, functools.partial(product_step, False), 0)
+    lax.fori_loop(1, k_tiles, functools.partial(product_step, False), 0)
 
     kept = parts * part_rows
     product_rows = product_out.reshape(parts * devices * part_rows, LANES)
@@ -216,6 +222,19 @@
 
         lax.fori_loop(0, n_row, pack, 0)
 
+    wait_for(block, block_recv)
+
+    batch = 4
+
+    def gate_step(b, carry):
+        some = pl.ds(b * batch, batch)
+        flat = block[some].reshape(batch * col_count, channels)
+        normed = norm(flat.astype(F32), g_in[...], 1)
+        gating = jnp.dot(normed, w_in[0, :, 4 * hidden :], preferred_element_type=F32)
+        gate[some] = jax.nn.sigmoid(gating).reshape(batch, col_count, channels)
+        return carry
+
+    lax.fori_loop(0, row_count // batch, gate_step, 0)
     product_in_rows = product_in.reshape(parts * devices * part_rows, LANES)
     for part in range(parts):
         wait_for(product_in.at[part], product_recv.at[part])
@@ -256,9 +275,13 @@
     return pl.pallas_call(
         functools.partial(kernel, n_row, n_col),
         out_shape=jax.ShapeDtypeStruct((1, row_count, col_count, channels), BF16),
-        in_specs=[pl.BlockSpec(memory_space=pl.ANY)] + [vmem] * 5,
+        in_specs=[pl.BlockSpec(memory_space=pl.ANY)] * 6,
         out_specs=vmem,
         scratch_shapes=[
+            pltpu.VMEM(input_weights.shape, BF16),
+            pltpu.VMEM(input_gain.shape, F32),
+            pltpu.VMEM(product_gain.shape, F32),
+            pltpu.VMEM(output_weights.shape, BF16),
             pltpu.VMEM((rows, size, channels), BF16),
             pltpu.VMEM((1, size), jnp.int32),
             pltpu.VMEM(input_weights.shape[:0:-1], BF16),
@@ -273,7 +296,7 @@
             pltpu.VMEM((devices * part_rows, LANES), F32),
             pltpu.VMEM((row_count, col_count, channels), BF16),
             pltpu.VMEM((row_count, col_count, channels), F32),
-            dma((2,)), dma, dma((k_tiles,)), dma, dma((k_tiles,)),
+            dma((4,)), dma((2,)), dma, dma((k_tiles,)), dma, dma((k_tiles,)),
             dma, dma((parts,)), dma, dma,
         ],
         compiler_params=pltpu.CompilerParams(

time: 138 us -> 118 us (0.86)
  Pallas kernels: 131 us -> 112 us
    pallas_call x1, Pallas kernels: 131 us -> 112 us  [local(): pl.pallas_call(functools.partial(kernel, n_row, n_col), out_shape=jax.Sha...]
where the time goes in v3:
time: 118 us
  Pallas kernels  112 us (95%)
  local copies, waits for them, and re-layouts  5.95 us (5%)
    pallas_call x1, Pallas kernels, local(): pl.pallas_call(functools.partial(kernel, n_row, n_col), out_shape=jax.Sha...  112 us
    unnamed x13, local copies, waits for them, and re-layouts  5.95 us

profile of v3, /device:TPU:1, one launch (start us, length us, event | category | flops | bytes accessed | tf_op | source)
XLA Modules:
  0.0 117.8 jit_solution(3423979966975291106)
XLA Ops:
  0.0 0.0 copy-start
  0.0 1.3 %copy-done = bf16[1,6,768,128]{3,2,1,0:T(8,128)(2,1)S(1)} copy-done((bf16[1,6,768,128]{3,2,1,0:T(8,128)(2,1)S(1)}, bf16[1,6,768,128]{3,2,1,0:T(8,128)(2,1)}, u32[]{:S(2)}) %copy-start) | copy-done | bytes 1179672
  1.3 0.0 copy-start.1
  1.3 0.9 copy-done.1
  2.2 0.0 copy-start.2
  2.2 0.8 copy-done.2
  2.9 0.0 copy-start.3
  2.9 0.7 copy-done.3
  3.6 0.0 copy-start.4
  3.6 0.7 copy-done.4
  4.3 0.0 copy-start.5
  4.3 0.7 copy-done.5
  4.9 111.8 %shard_map.64 = bf16[1,48,96,128]{3,2,1,0:T(8,128)(2,1)S(1)} custom-call(bf16[1,6,768,128]{3,2,1,0:T(8,128)(2,1)S(1)} %copy-done, s32[1,768]{1,0:T(1,128)S(1)} %copy-done.3, bf16[1,128,640]{2,1,0:T(8,128)(2,1)S(1)} %copy-done.1, f32[1,128]{1,0:T(1,128)S(1)} %copy-done.4, f32[1,128]{1,0:T(1,128)S(1)} %copy-done.5, bf16[1,128,128]{2,1,0:T(8,128)(2,1)S(1)} %copy-done.2), custom_call_target="tpu_custom_call" | custom-call | tf_op jit(solution)/shard_map/pallas_call | solution.py:275
  116.8 1.0 copy.8
Async XLA Ops:
  0.0 1.3 %copy-start = (bf16[1,6,768,128]{3,2,1,0:T(8,128)(2,1)S(1)}, bf16[1,6,768,128]{3,2,1,0:T(8,128)(2,1)}, u32[]{:S(2)}) copy-start(bf16[1,6,768,128]{3,2,1,0:T(8,128)(2,1)} %handed.1) | copy-start | bytes 3538948
  1.3 0.9 copy-start.1
  2.2 0.8 copy-start.2
  2.9 0.7 copy-start.3
  3.6 0.7 copy-start.4
  4.3 0.7 copy-start.5

commit v4 on v3

--- a/solution.py
+++ b/solution.py
@@ -30,7 +30,7 @@
     handed, mask, w_in_hbm, g_in_hbm, g_prod_hbm, w_out_hbm, out,
     w_in, g_in, g_prod, w_out, slab, flags, w_cols, g_cols, factor_f32, factor_out, factors, products,
     packed_f32, product_out, product_in, product_f32, block, gate,
-    load_sems, flag_sems, slab_send, slab_recv, factor_send, factor_recv,
+    load_sems, flag_sems, slab_send, slab_recv, factor_send, factor_recv, twin_send, twin_recv,
     product_send, product_recv, block_send, block_recv,
 ):
     rows, size, channels = slab.shape
@@ -38,13 +38,25 @@
     k_tiles = size // LANES
     devices = n_row * n_col
     row_count, col_count = size // n_row, size // n_col
-    parts, _, part_rows = product_out.shape[0], 0, 2 * product_out.shape[2]
+    parts, part_rows = product_out.shape[0], 2 * product_out.shape[2]
     section, row, col = (lax.axis_index(a) for a in ("section", "row", "col"))
     me = row * n_col + col
-    partner = (1 - section, row, col)
-
-    def at(t):
-        return (section, t // n_col, lax.rem(t, n_col))
+
+    ring = n_row // 2
+    half = ring // 2
+    plane, side_y, core = row // 2, lax.rem(row, 2), lax.rem(col, 2)
+
+    held_row = plane * 2 + 1 - side_y
+    partner = (1 - section, held_row, col)
+
+    def pair_base(z, c):
+        return lax.rem(lax.rem(z - c + ring, ring) // 2 * 2 + c, ring)
+
+    base = pair_base(plane, core)
+    upper = lax.rem(plane - base + ring, ring)
+    first_plane = lax.rem(base + half * upper + ring + 1 - half, ring)
+    twin = (section, lax.rem(base + 1 - upper, ring) * 2 + side_y, col)
+    own_channels = [(lax.rem(base + i, ring) * 2 + side_y) * n_col + col for i in range(2)]
 
     loads = [
         pltpu.make_async_copy(source, target, load_sems.at[i])
@@ -58,10 +70,16 @@
     pl.semaphore_signal(barrier, inc=1, device_id=partner, device_id_type=MESH)
 
     def greet(d, carry):
-        pl.semaphore_signal(barrier, inc=1, device_id=at(lax.rem(me + d, devices)), device_id_type=MESH)
-        return carry
-
-    lax.fori_loop(1, devices, greet, 0)
+        for e in range(n_col):
+            r, c = lax.rem(row + d, n_row), lax.rem(col + e, n_col)
+
+            @pl.when((d > 0) | (e > 0))
+            def _():
+                pl.semaphore_signal(barrier, inc=1, device_id=(section, r, c), device_id_type=MESH)
+
+        return carry
+
+    lax.fori_loop(0, n_row, greet, 0)
     for load in loads:
         load.wait()
     w_cols[...] = w_in[0].astype(F32).T.astype(BF16)
@@ -93,19 +111,13 @@
 
     block_rows = block.at[pl.ds(col * rows, rows)]
 
-    def send_block(c, carry):
-        @pl.when(c != col)
-        def _():
-            pltpu.make_async_remote_copy(
-                src_ref=slab.at[:, columns(c)], dst_ref=block_rows,
-                send_sem=block_send, recv_sem=block_recv,
-                device_id=(section, row, c), device_id_type=MESH,
-            ).start()
-
-        @pl.when(c == col)
-        def _():
-            pltpu.make_async_copy(slab.at[:, columns(c)], block_rows, block_recv).start()
-
+    def send_block(d, carry):
+        c = lax.rem(col + d, n_col)
+        pltpu.make_async_remote_copy(
+            src_ref=slab.at[:, columns(c)], dst_ref=block_rows,
+            send_sem=block_send, recv_sem=block_recv,
+            device_id=(section, held_row, c), device_id_type=MESH,
+        ).start()
         return carry
 
     per_owner = 2 * rows
@@ -113,7 +125,7 @@
     all_flags = flags[...].astype(F32)
     places = lax.broadcasted_iota(jnp.int32, all_flags.shape, 1)
     own_flags = [
-        jnp.sum(jnp.where(places == me * rows + i, all_flags, 0.0), axis=1, keepdims=True)
+        jnp.sum(jnp.where(places == (held_row * n_col + col) * rows + i, all_flags, 0.0), axis=1, keepdims=True)
         for i in range(rows)
     ]
 
@@ -139,88 +151,146 @@
                 )
         begin = pl.multiple_of(kt * (devices * per_owner), devices * per_owner)
         factor_rows[pl.ds(begin, devices * per_owner), :] = factor_f32[...].astype(BF16)
-        target = factors.at[:, kt, pl.ds(me * (rows // 2), rows // 2)]
-        pltpu.make_async_copy(factor_out.at[kt, me], target, factor_recv.at[kt]).start()
 
         def send(d, c):
-            t = lax.rem(me + d, devices)
-            pltpu.make_async_remote_copy(
-                src_ref=factor_out.at[kt, t], dst_ref=target,
-                send_sem=factor_send, recv_sem=factor_recv.at[kt],
-                device_id=at(t), device_id_type=MESH,
-            ).start()
+            r = lax.rem(row + d, n_row)
+            for parity in range(2):
+                z = r // 2
+                low = pair_base(z, lax.rem(core + parity, 2))
+                turn = lax.rem(plane - low + half - 1 + ring, ring)
+                near = lax.rem(low + turn // half, ring) * 2 + lax.rem(r, 2)
+                place = (lax.rem(turn, half) * 2 + 1 - side_y) * n_col + col
+                target = factors.at[
+                    pl.ds(0, 2), lax.rem(z - low + ring, ring), kt, pl.ds(place * (rows // 2), rows // 2)
+                ]
+                for e in range(parity, n_col, 2):
+                    channel_col = lax.rem(col + e, n_col)
+                    source = factor_out.at[kt, r * n_col + channel_col]
+
+                    def remote(source=source, target=target, near=near, channel_col=channel_col):
+                        pltpu.make_async_remote_copy(
+                            src_ref=source, dst_ref=target,
+                            send_sem=factor_send, recv_sem=factor_recv.at[kt],
+                            device_id=(section, near, channel_col), device_id_type=MESH,
+                        ).start()
+
+                    if e:
+                        remote()
+                    else:
+                        pl.when(near != row)(remote)
+
+                        @pl.when(near == row)
+                        def _(source=source, target=target):
+                            pltpu.make_async_copy(source, target, factor_recv.at[kt]).start()
+
             return c
 
-        lax.fori_loop(1, devices, send, 0)
+        lax.fori_loop(0, n_row, send, 0)
         return carry
 
     lax.fori_loop(0, k_tiles, factor_step, 0)
 
-    def send_block_turn(d, carry):
-        return send_block(lax.rem(col + d, n_col), carry)
-
-    lax.fori_loop(0, n_col, send_block_turn, 0)
-
-    arrived = factors.reshape(2 * k_tiles * size, LANES)
-    strip = 256
-
-    def product_step(first, kt, carry):
-        wait_for(factors.at[:, kt], factor_recv.at[kt])
-        right = arrived[pl.ds(pl.multiple_of((k_tiles + kt) * size, size), size), :]
-        for m in range(0, size, strip):
-            left = arrived[pl.ds(pl.multiple_of(kt * size + m, strip), strip), :]
-            part = lax.dot_general(left, right, (((1,), (1,)), ((), ())), preferred_element_type=F32)
-            products[m : m + strip, :] = part if first else products[m : m + strip, :] + part
-        return carry
-
+    lax.fori_loop(0, n_col, send_block, 0)
+
+    span = size // 2
+    arrived = factors.reshape(3 * 2 * k_tiles * span, LANES)
+
+    def product_step(first, which, kt):
+        for channel in range(2):
+            def operand(kind):
+                begin = ((kind * 2 + channel) * k_tiles + kt) * span
+                return arrived[pl.ds(pl.multiple_of(begin, span), span), :]
+
+            part = lax.dot_general(
+                operand(0), operand(1 + which), (((1,), (1,)), ((), ())), preferred_element_type=F32
+            )
+            spot = (slice(channel * span, (channel + 1) * span), slice(which * span, (which + 1) * span))
+            products[spot] = part if first else products[spot] + part
+
+    def twin_copy(kt):
+        return pltpu.make_async_remote_copy(
+            src_ref=factors.at[1, :, kt], dst_ref=factors.at[2, :, kt],
+            send_sem=twin_send, recv_sem=twin_recv.at[kt],
+            device_id=twin, device_id_type=MESH,
+        )
+
+    def take(kt):
+        wait_for(factors.at[pl.ds(0, 2), :, kt], factor_recv.at[kt])
+        twin_copy(kt).start()
+
+    def take_twin(kt):
+        wait_for(factors.at[2, :, kt], twin_recv.at[kt])
+
+    def product_steps(kt, carry):
+        take(kt)
+        product_step(False, 0, kt)
+        take_twin(kt - 1)
+        product_step(False, 1, kt - 1)
+        return carry
+
+    take(0)
     product_step(True, 0, 0)
-    lax.fori_loop(1, k_tiles, functools.partial(product_step, False), 0)
+    take(1)
+    product_step(False, 0, 1)
+    take_twin(0)
+    product_step(True, 1, 0)
+    lax.fori_loop(2, k_tiles, product_steps, 0)
 
     kept = parts * part_rows
     product_rows = product_out.reshape(parts * devices * part_rows, LANES)
     spare = LANES - col_count
 
-    for part in range(parts):
-
-        def pack(d, carry, part=part):
-            r = lax.rem(row + d, n_row)
-            tile_rows = products[pl.ds(pl.multiple_of(r * row_count, row_count), row_count), :]
-            for c in range(n_col):
+    def pack(part, begin_block, end_block):
+        blocks = end_block - begin_block
+
+        def step(d, carry):
+            channel, group = lax.rem(d, 2), d // 2
+            tile_rows = products[
+                pl.ds(pl.multiple_of(channel * span + group * row_count, row_count), row_count),
+                begin_block * col_count : end_block * col_count,
+            ]
+            for c in range(blocks):
                 into = slice(c * part_rows, (c + 1) * part_rows)
                 packed_f32[into, :col_count] = tile_rows[
                     part * part_rows : (part + 1) * part_rows, c * col_count : (c + 1) * col_count
                 ]
                 begin = c * col_count + part * spare
                 packed_f32[into, col_count:] = tile_rows[kept:, begin : begin + spare]
-            base = part * devices + r * n_col
-            product_rows[pl.ds(pl.multiple_of(base * part_rows, n_col * part_rows), n_col * part_rows), :] = (
-                packed_f32[...].astype(BF16)
+            index = (channel * n_col + group) * n_col + begin_block
+            begin = (part * devices + index) * part_rows
+            product_rows[pl.ds(pl.multiple_of(begin, 4 * part_rows), blocks * part_rows), :] = (
+                packed_f32[: blocks * part_rows, :].astype(BF16)
             )
-
-            def send(e, cc):
-                c = lax.rem(col + e, n_col)
-                t = r * n_col + c
-
-                @pl.when(t != me)
-                def _():
+            r = lax.rem(first_plane + group // 2, ring) * 2 + lax.rem(group, 2)
+            own = own_channels[0] + channel * (own_channels[1] - own_channels[0])
+            for m in range(begin_block, end_block):
+                c = lax.rem(first_plane + m, n_col)
+                source = product_out.at[part, index + (m - begin_block)]
+                target = product_in.at[part, own]
+                here = (r == row) & (c == col)
+
+                @pl.when(jnp.logical_not(here))
+                def _(source=source, target=target, c=c):
                     pltpu.make_async_remote_copy(
-                        src_ref=product_out.at[part, t], dst_ref=product_in.at[part, me],
+                        src_ref=source, dst_ref=target,
                         send_sem=product_send, recv_sem=product_recv.at[part],
                         device_id=(section, r, c), device_id_type=MESH,
                     ).start()
 
-                @pl.when(t == me)
-                def _():
-                    pltpu.make_async_copy(
-                        product_out.at[part, me], product_in.at[part, me], product_recv.at[part]
-                    ).start()
-
-                return cc
-
-            lax.fori_loop(0, n_col, send, 0)
+                @pl.when(here)
+                def _(source=source, target=target):
+                    pltpu.make_async_copy(source, target, product_recv.at[part]).start()
+
             return carry
 
-        lax.fori_loop(0, n_row, pack, 0)
+        lax.fori_loop(0, n_row, step, 0)
+
+    pack(0, 0, n_col // 2)
+    take_twin(k_tiles - 1)
+    product_step(False, 1, k_tiles - 1)
+    pack(0, n_col // 2, n_col)
+    for part in range(1, parts):
+        pack(part, 0, n_col)
 
     wait_for(block, block_recv)
 
@@ -256,9 +326,10 @@
         lax.fori_loop(0, part_rows, finish, 0)
 
     wait_for(slab, slab_send)
-    wait_for(factor_out.at[:, pl.ds(0, devices - 1)], factor_send)
-    wait_for(product_out.at[:, pl.ds(0, devices - 1)], product_send)
-    wait_for(block.at[pl.ds(0, (n_col - 1) * rows)], block_send)
+    wait_for(factor_out.at[:, pl.ds(0, devices - 2)], factor_send)
+    wait_for(factors.at[1], twin_send)
+    wait_for(product_out.at[:, pl.ds(0, devices - 2)], product_send)
+    wait_for(block, block_send)
 
 
 def local(n_row, n_col, handed, residue_mask, input_weights, input_gain, product_gain, output_weights):
@@ -288,7 +359,7 @@
             pltpu.VMEM((hidden, LANES), F32),
             pltpu.VMEM((devices * 2 * rows, LANES), F32),
             pltpu.VMEM((k_tiles, devices, 2, rows // 2, 2, LANES), BF16),
-            pltpu.VMEM((2, k_tiles, size // 2, 2, LANES), BF16),
+            pltpu.VMEM((3, 2, k_tiles, size // 4, 2, LANES), BF16),
             pltpu.VMEM((size, size), F32),
             pltpu.VMEM((n_col * part_rows, LANES), F32),
             pltpu.VMEM((parts, devices, part_rows // 2, 2, LANES), BF16),
@@ -297,7 +368,7 @@
             pltpu.VMEM((row_count, col_count, channels), BF16),
             pltpu.VMEM((row_count, col_count, channels), F32),
             dma((4,)), dma((2,)), dma, dma((k_tiles,)), dma, dma((k_tiles,)),
-            dma, dma((parts,)), dma, dma,
+            dma, dma((k_tiles,)), dma, dma((parts,)), dma, dma,
         ],
         compiler_params=pltpu.CompilerParams(
             collective_id=0, has_side_effects=True, vmem_limit_bytes=48 * 2**20

time: 118 us -> 109 us (0.924)
  Pallas kernels: 112 us -> 103 us
    pallas_call x1, Pallas kernels: 112 us -> 103 us  [local(): pl.pallas_call(functools.partial(kernel, n_row, n_col), out_shape=jax.Sha...]
where the time goes in v4:
time: 109 us
  Pallas kernels  103 us (94%)
  local copies, waits for them, and re-layouts  5.95 us (5%)
    pallas_call x1, Pallas kernels, local(): pl.pallas_call(functools.partial(kernel, n_row, n_col), out_shape=jax.Sha...  103 us
    unnamed x13, local copies, waits for them, and re-layouts  5.95 us

profile of v4, /device:TPU:1, one launch (start us, length us, event | category | flops | bytes accessed | tf_op | source)
XLA Modules:
  0.0 109.0 jit_solution(2154122470132024936)
XLA Ops:
  0.0 0.0 copy-start
  0.0 1.3 %copy-done = bf16[1,6,768,128]{3,2,1,0:T(8,128)(2,1)S(1)} copy-done((bf16[1,6,768,128]{3,2,1,0:T(8,128)(2,1)S(1)}, bf16[1,6,768,128]{3,2,1,0:T(8,128)(2,1)}, u32[]{:S(2)}) %copy-start) | copy-done | bytes 1179672
  1.3 0.0 copy-start.1
  1.3 0.9 copy-done.1
  2.2 0.0 copy-start.2
  2.2 0.8 copy-done.2
  2.9 0.0 copy-start.3
  2.9 0.7 copy-done.3
  3.6 0.0 copy-start.4
  3.6 0.7 copy-done.4
  4.3 0.0 copy-start.5
  4.3 0.7 copy-done.5
  4.9 103.0 %shard_map.64 = bf16[1,48,96,128]{3,2,1,0:T(8,128)(2,1)S(1)} custom-call(bf16[1,6,768,128]{3,2,1,0:T(8,128)(2,1)S(1)} %copy-done, s32[1,768]{1,0:T(1,128)S(1)} %copy-done.3, bf16[1,128,640]{2,1,0:T(8,128)(2,1)S(1)} %copy-done.1, f32[1,128]{1,0:T(1,128)S(1)} %copy-done.4, f32[1,128]{1,0:T(1,128)S(1)} %copy-done.5, bf16[1,128,128]{2,1,0:T(8,128)(2,1)S(1)} %copy-done.2), custom_call_target="tpu_custom_call" | custom-call | tf_op jit(solution)/shard_map/pallas_call | solution.py:346
  108.0 1.0 copy.8
Async XLA Ops:
  0.0 1.3 %copy-start = (bf16[1,6,768,128]{3,2,1,0:T(8,128)(2,1)S(1)}, bf16[1,6,768,128]{3,2,1,0:T(8,128)(2,1)}, u32[]{:S(2)}) copy-start(bf16[1,6,768,128]{3,2,1,0:T(8,128)(2,1)} %handed.1) | copy-start | bytes 3538948
  1.3 0.9 copy-start.1
  2.2 0.8 copy-start.2
  2.9 0.7 copy-start.3
  3.6 0.7 copy-start.4
  4.3 0.7 copy-start.5

commit v5 on v4

--- a/solution.py
+++ b/solution.py
@@ -371,7 +371,7 @@
             dma, dma((k_tiles,)), dma, dma((parts,)), dma, dma,
         ],
         compiler_params=pltpu.CompilerParams(
-            collective_id=0, has_side_effects=True, vmem_limit_bytes=48 * 2**20
+            collective_id=0, has_side_effects=True, vmem_limit_bytes=61 * 2**20
         ),
     )(handed, residue_mask, input_weights, input_gain, product_gain, output_weights)
 

time: 109 us -> 106 us (0.972)
  local copies, waits for them, and re-layouts: 5.95 us -> 2.36 us
    unnamed x13 -> x1, local copies, waits for them, and re-layouts: 5.95 us -> 2.36 us
where the time goes in v5:
time: 106 us
  Pallas kernels  104 us (98%)
  local copies, waits for them, and re-layouts  2.36 us (2%)
    pallas_call x1, Pallas kernels, local(): pl.pallas_call(functools.partial(kernel, n_row, n_col), out_shape=jax.Sha...  104 us
    unnamed x1, local copies, waits for them, and re-layouts  2.36 us

profile of v5, /device:TPU:1, one launch (start us, length us, event | category | flops | bytes accessed | tf_op | source)
XLA Modules:
  0.0 106.3 jit_solution(12175396484932862077)
XLA Ops:
  0.0 104.0 %shard_map.64 = bf16[1,48,96,128]{3,2,1,0:T(8,128)(2,1)} custom-call(bf16[1,6,768,128]{3,2,1,0:T(8,128)(2,1)} %handed.1, s32[1,768]{1,0:T(1,128)} %mask.1, bf16[1,128,640]{2,1,0:T(8,128)(2,1)} %w_in_hbm.1, f32[1,128]{1,0:T(1,128)} %g_in_hbm.1, f32[1,128]{1,0:T(1,128)} %g_prod_hbm.1, bf16[1,128,128]{2,1,0:T(8,128)(2,1)} %w_out_hbm.1), custom_call_target="tpu_custom_call" | custom-call | tf_op jit(solution)/shard_map/pallas_call | solution.py:346
  104.0 2.4 %copy.8 = bf16[1,48,96,128]{3,2,1,0:T(8,128)(2,1)} copy(bf16[1,48,96,128]{3,2,1,0:T(8,128)(2,1)} %shard_map.64) | data formatting | bytes 2359296

commit v6 on v5

--- a/solution.py
+++ b/solution.py
@@ -323,7 +323,7 @@
             out[0, i, j] = (block[i, j].astype(F32) + gate[i, j] * update[col_count:]).astype(BF16)
             return carry
 
-        lax.fori_loop(0, part_rows, finish, 0)
+        lax.fori_loop(0, part_rows, finish, 0, unroll=6)
 
     wait_for(slab, slab_send)
     wait_for(factor_out.at[:, pl.ds(0, devices - 2)], factor_send)

time: 106 us -> 104 us (0.981)
  Pallas kernels: 104 us -> 102 us
    pallas_call x1, Pallas kernels: 104 us -> 102 us  [local(): pl.pallas_call(functools.partial(kernel, n_row, n_col), out_shape=jax.Sha...]
where the time goes in v6:
time: 104 us
  Pallas kernels  102 us (98%)
  local copies, waits for them, and re-layouts  2.36 us (2%)
    pallas_call x1, Pallas kernels, local(): pl.pallas_call(functools.partial(kernel, n_row, n_col), out_shape=jax.Sha...  102 us
    unnamed x1, local copies, waits for them, and re-layouts  2.36 us

profile of v6, /device:TPU:1, one launch (start us, length us, event | category | flops | bytes accessed | tf_op | source)
XLA Modules:
  0.0 104.0 jit_solution(13006946370344723036)
XLA Ops:
  0.0 101.6 %shard_map.64 = bf16[1,48,96,128]{3,2,1,0:T(8,128)(2,1)} custom-call(bf16[1,6,768,128]{3,2,1,0:T(8,128)(2,1)} %handed.1, s32[1,768]{1,0:T(1,128)} %mask.1, bf16[1,128,640]{2,1,0:T(8,128)(2,1)} %w_in_hbm.1, f32[1,128]{1,0:T(1,128)} %g_in_hbm.1, f32[1,128]{1,0:T(1,128)} %g_prod_hbm.1, bf16[1,128,128]{2,1,0:T(8,128)(2,1)} %w_out_hbm.1), custom_call_target="tpu_custom_call" | custom-call | tf_op jit(solution)/shard_map/pallas_call | solution.py:346
  101.6 2.4 %copy.8 = bf16[1,48,96,128]{3,2,1,0:T(8,128)(2,1)} copy(bf16[1,48,96,128]{3,2,1,0:T(8,128)(2,1)} %shard_map.64) | data formatting | bytes 2359296
